TPU v7x, 32 devices: a whole 2x2x4 slice. The times are simulated.
32 devices in a mesh: row: 8 (over y, x, core), col: 4 (over z).
Axes of the slice: x: 2, y: 2, z: 4, core: 2. Of those that a mesh axis runs over, the one named last changes fastest.
Arguments:
- inputs: bfloat16 [128, 12288], P('col', 'row'), may hold values from -6 to 6
- up_weight: bfloat16 [12288, 24576], P('row', 'col'), may hold values from -0.0546875 to 0.0546875
- down_weight: bfloat16 [24576, 12288], P('col', 'row'), may hold values from -0.078125 to 0.078125
- cotangent: bfloat16 [128, 12288], P('col', 'row'), may hold values from -6 to 6
Outputs:
- outputs: bfloat16 [128, 12288], P('col', 'row')
- input_grad: bfloat16 [128, 12288], P('col', 'row')
- up_grad: bfloat16 [12288, 24576], P('row', 'col')
- down_grad: bfloat16 [24576, 12288], P('col', 'row')
All inputs are finite; a program needn't handle non-finite values.
Results may differ from a plain program's by a relative error of at most 0.005.
Values may be sent and summed in bfloat16 or wider, within the bound.
A program may use at most 128 MiB of HBM per device.

v0:
```python
import math

import jax
import jax.numpy as jnp
from jax import lax
from jax.sharding import PartitionSpec as P


def gelu_value(v):
    cval = math.sqrt(2.0 / math.pi)
    return 0.5 * v * (1.0 + jnp.tanh(cval * (v + 0.044715 * v * v * v)))


def gelu_slope(v):
    cval = math.sqrt(2.0 / math.pi)
    tval = jnp.tanh(cval * (v + 0.044715 * v * v * v))
    return 0.5 * (1.0 + tval) + 0.5 * v * (1.0 - tval * tval) * cval * (
        1.0 + 3.0 * 0.044715 * v * v
    )


def times_transposed(left, right):
    return lax.dot_general(
        left, right, (((1,), (1,)), ((), ())), preferred_element_type=jnp.float32
    )


def over_tokens(left, right):
    return lax.dot_general(
        left, right, (((0,), (0,)), ((), ())), preferred_element_type=jnp.float32
    )


def per_device(inputs, up_weight, down_weight, cotangent):
    all_inputs = lax.all_gather(inputs, "col", axis=0, tiled=True)
    all_cotangent = lax.all_gather(cotangent, "col", axis=0, tiled=True)
    preact = lax.psum_scatter(
        jnp.dot(all_inputs, up_weight, preferred_element_type=jnp.float32),
        "row",
        scatter_dimension=0,
        tiled=True,
    )
    activ = gelu_value(preact).astype(jnp.bfloat16)
    all_activ = lax.all_gather(activ, "row", axis=0, tiled=True)
    outputs = lax.psum_scatter(
        jnp.dot(all_activ, down_weight, preferred_element_type=jnp.float32),
        "col",
        scatter_dimension=0,
        tiled=True,
    ).astype(jnp.bfloat16)
    act_grad = lax.psum_scatter(
        times_transposed(all_cotangent, down_weight), "row", scatter_dimension=0, tiled=True
    )
    pre_grad = (act_grad * gelu_slope(preact)).astype(jnp.bfloat16)
    all_pregrad = lax.all_gather(pre_grad, "row", axis=0, tiled=True)
    down_grad = over_tokens(all_activ, all_cotangent).astype(jnp.bfloat16)
    up_grad = over_tokens(all_inputs, all_pregrad).astype(jnp.bfloat16)
    input_grad = lax.psum_scatter(
        times_transposed(all_pregrad, up_weight), "col", scatter_dimension=0, tiled=True
    ).astype(jnp.bfloat16)
    return (outputs, input_grad, up_grad, down_grad)


def solution(mesh):
    placed = (P("col", "row"), P("row", "col"), P("col", "row"), P("col", "row"))
    return jax.shard_map(
        per_device,
        mesh=mesh,
        in_specs=placed,
        out_specs=(P("col", "row"), P("col", "row"), P("row", "col"), P("col", "row")),
        check_vma=False,
    )
```

profile of v0, /device:TPU:0, one launch (start us, length us, event | category | flops | bytes accessed | tf_op | source)
XLA Modules:
  0.0 260.8 jit_solution(11959995784834750752)
XLA Ops:
  7.2 0.0 reduce-scatter.9.cloned.1.call-start
  7.2 16.4 %all_gather.14 = bf16[128,1536]{1,0:T(8,128)(2,1)S(1)} all-gather(bf16[32,1536]{1,0:T(8,128)(2,1)} %param.7), channel_id=1, replica_groups=mesh['row'=8,'col'=4] {'col'}, dimensions={0}, use_global_device_ids=true | all-gather | bytes 491520 | tf_op jit(solution)/shard_map/all_gather | solution.py:36
  23.7 14.1 %fusion.10 = f32[128,6144]{1,0:T(8,128)} fusion(bf16[128,1536]{1,0:T(8,128)(2,1)S(1)} %all_gather.14, bf16[6144,1536]{1,0:T(8,128)(2,1)} %param.6), kind=kOutput, calls=%fused_computation.15 | convolution fusion | flops 2415919104 | bytes 22413312 | tf_op jit(solution)/shard_map/dot_general | solution.py:23
  37.8 0.0 reduce-scatter.5.cloned.1.call-start
  37.8 15.4 %all_gather.12 = bf16[128,1536]{1,0:T(8,128)(2,1)S(1)} all-gather(bf16[32,1536]{1,0:T(8,128)(2,1)S(1)} %copy-done.2), channel_id=1, replica_groups=mesh['row'=8,'col'=4] {'col'}, dimensions={0}, use_global_device_ids=true | all-gather | bytes 491520 | tf_op jit(solution)/shard_map/all_gather | solution.py:35
  53.3 10.7 %fusion.8 = f32[128,6144]{1,0:T(8,128)} fusion(bf16[128,1536]{1,0:T(8,128)(2,1)S(1)} %all_gather.12, bf16[1536,6144]{1,0:T(8,128)(2,1)} %param.5), kind=kOutput, calls=%fused_computation.13 | convolution fusion | flops 2415919104 | bytes 22413312 | tf_op jit(solution)/shard_map/dot_general | solution.py:38
  63.9 0.0 all-gather.3.cloned.1.call-start
  64.0 21.9 %reduce-scatter.9.cloned.1.call-done = f32[16,6144]{1,0:T(8,128)} async-done(((f32[128,6144]{1,0:T(8,128)}), f32[16,6144]{1,0:T(8,128)}) %reduce-scatter.9.cloned.1.call-update) | async-done | bytes 393232 | tf_op jit(solution)/shard_map/reduce_scatter | solution.py:51
  85.9 50.6 %reduce-scatter.5.cloned.1.call-done = f32[16,6144]{1,0:T(8,128)} async-done(((f32[128,6144]{1,0:T(8,128)}), f32[16,6144]{1,0:T(8,128)}) %reduce-scatter.5.cloned.1.call-update) | async-done | bytes 393232 | tf_op jit(solution)/shard_map/reduce_scatter | solution.py:37
  136.5 2.1 fusion.7
  138.7 0.0 all-gather.3.cloned.1.call-update
  138.7 0.0 all-gather.5.cloned.1.call-start
  138.7 0.5 all-gather.5.cloned.1.call-update
  139.3 0.0 reduce-scatter.7.cloned.1.call-start
  139.3 25.4 %all-gather.3.cloned.1.call-done = bf16[128,6144]{1,0:T(8,128)(2,1)} async-done(((bf16[16,6144]{1,0:T(8,128)(2,1)}), bf16[128,6144]{1,0:T(8,128)(2,1)}) %all-gather.3.cloned.1.call-update) | async-done | bytes 1572880 | tf_op jit(solution)/shard_map/all_gather | solution.py:44
  164.7 10.4 %fusion.9 = f32[128,1536]{1,0:T(8,128)} fusion(bf16[128,6144]{1,0:T(8,128)(2,1)} %all-gather.3.cloned.1.call-done, bf16[6144,1536]{1,0:T(8,128)(2,1)} %param.6), kind=kOutput, calls=%fused_computation.14 | convolution fusion | flops 2415919104 | bytes 21233664 | tf_op jit(solution)/shard_map/dot_general | solution.py:46
  175.1 0.2 reduce-scatter.11.cloned.1.call-start
  175.3 17.4 %all-gather.5.cloned.1.call-done = bf16[128,6144]{1,0:T(8,128)(2,1)} async-done(((bf16[16,6144]{1,0:T(8,128)(2,1)}), bf16[128,6144]{1,0:T(8,128)(2,1)}) %all-gather.5.cloned.1.call-update) | async-done | bytes 1572880 | tf_op jit(solution)/shard_map/all_gather | solution.py:55
  192.8 14.2 %fusion.11 = f32[128,1536]{1,0:T(8,128)} fusion(bf16[128,6144]{1,0:T(8,128)(2,1)} %all-gather.5.cloned.1.call-done, bf16[1536,6144]{1,0:T(8,128)(2,1)} %param.5), kind=kOutput, calls=%fused_computation.16 | convolution fusion | flops 2415919104 | bytes 21233664 | tf_op jit(solution)/shard_map/dot_general | solution.py:23
  207.0 9.5 %fusion = bf16[1536,6144]{0,1:T(8,128)(2,1)} fusion(bf16[128,6144]{1,0:T(8,128)(2,1)S(1)} %copy-done.1, bf16[128,1536]{1,0:T(8,128)(2,1)S(1)} %all_gather.12), kind=kOutput, calls=%fused_computation.2 | convolution fusion | flops 2425356288 | bytes 20840448 | tf_op jit(solution)/shard_map/dot_general | solution.py:29
  216.5 24.7 %copy.8 = bf16[1536,6144]{1,0:T(8,128)(2,1)} copy(bf16[1536,6144]{0,1:T(8,128)(2,1)} %fusion) | data formatting | bytes 37748736
  241.3 9.5 %convolution_convert_fusion = bf16[6144,1536]{1,0:T(8,128)(2,1)} fusion(bf16[128,6144]{1,0:T(8,128)(2,1)S(1)} %copy-done, bf16[128,1536]{1,0:T(8,128)(2,1)S(1)} %all_gather.14), kind=kOutput, calls=%fused_computation | convolution fusion | flops 2425356288 | bytes 20840448 | tf_op jit(solution)/shard_map/dot_general | solution.py:29
  250.8 1.6 convert_element_type.22
  252.3 1.6 convert_element_type.24
  (12 shorter events, 0.1 us)
Async XLA Ops:
  7.2 78.8 %reduce-scatter.9.cloned.1.call-start = ((), (), s32[]{:S(2)}) async-start(), calls=%async_computation.7 | async-start | bytes 3538944 | tf_op jit(solution)/shard_map/reduce_scatter | solution.py:51
  23.7 14.2 %copy-start.2 = (bf16[32,1536]{1,0:T(8,128)(2,1)S(1)}, bf16[32,1536]{1,0:T(8,128)(2,1)}, u32[]{:S(2)}) copy-start(bf16[32,1536]{1,0:T(8,128)(2,1)} %param.4) | copy-start | bytes 294916
  37.8 98.8 %reduce-scatter.5.cloned.1.call-start = ((), (), s32[]{:S(2)}) async-start(), calls=%async_computation.4 | async-start | bytes 3538944 | tf_op jit(solution)/shard_map/reduce_scatter | solution.py:37
  63.9 100.8 %all-gather.3.cloned.1.call-start = ((), (), s32[]{:S(2)}) async-start(), calls=%async_computation.5 | async-start | bytes 1769472 | tf_op jit(solution)/shard_map/all_gather | solution.py:44
  138.7 54.1 %all-gather.5.cloned.1.call-start = ((), (), s32[]{:S(2)}) async-start(), calls=%async_computation.8 | async-start | bytes 1769472 | tf_op jit(solution)/shard_map/all_gather | solution.py:55
  139.3 111.5 %reduce-scatter.7.cloned.1.call-start = ((), (), s32[]{:S(2)}) async-start(), calls=%async_computation.6 | async-start | bytes 983040 | tf_op jit(solution)/shard_map/reduce_scatter | solution.py:45
  175.1 77.2 %reduce-scatter.11.cloned.1.call-start = ((), (), s32[]{:S(2)}) async-start(), calls=%async_computation.9 | async-start | bytes 983040 | tf_op jit(solution)/shard_map/reduce_scatter | solution.py:58
  192.8 14.2 %copy-start.1 = (bf16[128,6144]{1,0:T(8,128)(2,1)S(1)}, bf16[128,6144]{1,0:T(8,128)(2,1)}, u32[]{:S(2)}) copy-start(bf16[128,6144]{1,0:T(8,128)(2,1)} %all-gather.5.cloned.1.call-done) | copy-start | bytes 4718596
  216.5 24.8 %copy-start = (bf16[128,6144]{1,0:T(8,128)(2,1)S(1)}, bf16[128,6144]{1,0:T(8,128)(2,1)}, u32[]{:S(2)}) copy-start(bf16[128,6144]{1,0:T(8,128)(2,1)} %all-gather.3.cloned.1.call-done) | copy-start | bytes 4718596
Sparse Core Ops, SparseCore 0:
  37.9 47.9 reduce-scatter.8
  90.2 46.2 reduce-scatter.4
  139.0 25.6 all-gather.2
  167.0 25.6 all-gather.4
  194.9 23.2 reduce-scatter.6
  220.4 22.6 reduce-scatter.10
where the time goes:
time: 262 us; the launch traced here: 261 us
  waiting for transfers between devices  116 us (44%)
  matrix products  68.3 us (26%)
  blocking collectives  31.9 us (12%)
  local copies, waits for them, and re-layouts  24.8 us (9%)
  between operations  14.1 us (5%)
  other arithmetic  5.28 us (2%)
    reduce_scatter x1, waiting for transfers between devices, per_device(): lax.psum_scatter(jnp.dot(all_inputs, up_weight, preferred_element_type=jn...  50.6 us
    dot_general x2, matrix products, times_transposed(): lax.dot_general(left, right, (((1,), (1,)), ((), ())), preferred_element_...  28.3 us
    all_gather x1, waiting for transfers between devices, per_device(): all_activ = lax.all_gather(activ, 'row', axis=0, tiled=True)  25.4 us
    unnamed x7, local copies, waits for them, and re-layouts  24.8 us
    reduce_scatter x1, waiting for transfers between devices, per_device(): lax.psum_scatter(times_transposed(all_cotangent, down_weight), 'row', sca...  21.9 us
    dot_general x2, matrix products, over_tokens(): lax.dot_general(left, right, (((0,), (0,)), ((), ())), preferred_element_...  19 us
    all_gather x1, waiting for transfers between devices, per_device(): all_pregrad = lax.all_gather(pre_grad, 'row', axis=0, tiled=True)  17.4 us
    all_gather x1, blocking collectives, per_device(): all_cotangent = lax.all_gather(cotangent, 'col', axis=0, tiled=True)  16.4 us
  transfers between devices with their start and end apart: 6, of which 4 were waited for; matrix products, arithmetic and copies ran while one was open for 31% of the time, Pallas kernels for 0%

commit v1 on v0

v1 whole, which is shorter than its diff:
```python
import functools
import math

import jax
import jax.numpy as jnp
from jax import lax
from jax.experimental import pallas as pl
from jax.experimental.pallas import tpu as pltpu
from jax.sharding import PartitionSpec as P

PARTS = 4
BF16 = jnp.bfloat16
F32 = jnp.float32


def gelu_value(v):
    cval = math.sqrt(2.0 / math.pi)
    return 0.5 * v * (1.0 + jnp.tanh(cval * (v + 0.044715 * v * v * v)))


def gelu_slope(v):
    cval = math.sqrt(2.0 / math.pi)
    tval = jnp.tanh(cval * (v + 0.044715 * v * v * v))
    return 0.5 * (1.0 + tval) + 0.5 * v * (1.0 - tval * tval) * cval * (
        1.0 + 3.0 * 0.044715 * v * v
    )


def times(left, right):
    return jnp.dot(left, right, preferred_element_type=F32)


def times_transposed(left, right):
    return lax.dot_general(
        left, right, (((1,), (1,)), ((), ())), preferred_element_type=F32
    )


def over_tokens(left, right):
    return lax.dot_general(
        left, right, (((0,), (0,)), ((), ())), preferred_element_type=F32
    )


def layer_kernel(
    rows, cols,
    x_ref, up_ref, down_ref, cot_ref,
    act_out, pg_out, x_out, cot_out, z_out,
    x_all, cot_all, wu, wd, part, pair_in, pair_sum, chip_in, preact, gathered,
    z_sum, z_low,
    w_sem, zs_sem, zr_sem, ps_sem, pr_sem, cs_sem, cr_sem, gs_sem, gr_sem,
    fs_sem, fr_sem, o_sem, xo_sem,
):
    chips = rows // 2
    tokens, width = x_all.shape
    share = x_ref.shape[0]
    half = tokens // 2
    own = tokens // rows
    cw = wu.shape[2]
    items = 2 * PARTS

    r = lax.axis_index("row")
    z = lax.axis_index("col")
    core = lax.rem(r, 2)
    chip = r // 2
    partner = {"row": r + 1 - 2 * core}

    def peer_chip(k):
        return lax.rem(chip + k, chips)

    def source_chip(k):
        return lax.rem(chip + chips - k, chips)

    def peer(k):
        return {"row": peer_chip(k) * 2 + core}

    def block(side, where):
        return pl.ds(pl.multiple_of(side * half + where * own, 16), own)

    def send(src, dst, s_sem, r_sem, to):
        return pltpu.make_async_remote_copy(
            src_ref=src, dst_ref=dst, send_sem=s_sem, recv_sem=r_sem,
            device_id=to, device_id_type=pl.DeviceIdType.MESH,
        )

    loads = []
    for t in range(2):
        for j in range(PARTS):
            if t == 0:
                cp = pltpu.make_async_copy(
                    up_ref.at[:, pl.ds(j * cw, cw)], wu.at[j], w_sem.at[0, j])
            else:
                cp = pltpu.make_async_copy(
                    down_ref.at[pl.ds(j * cw, cw), :], wd.at[j], w_sem.at[1, j])
            cp.start()
            loads.append(cp)

    barrier = pltpu.get_barrier_semaphore()
    mates = [partner] + [peer(k) for k in range(1, chips)]
    mates += [{"col": lax.rem(z + k, cols)} for k in range(1, cols)]
    for mate in mates:
        pl.semaphore_signal(
            barrier, inc=1, device_id=mate, device_id_type=pl.DeviceIdType.MESH)
    mine = pl.ds(pl.multiple_of(z * share, 16), share)
    x_all[mine, :] = x_ref[...]
    cot_all[mine, :] = cot_ref[...]
    pl.semaphore_wait(barrier, len(mates))

    z_copies = [[], []]
    for t, (ref, whole) in enumerate(((x_ref, x_all), (cot_ref, cot_all))):
        for k in range(1, cols):
            z_copies[t].append(send(
                ref, whole.at[mine, :], zs_sem.at[t, k - 1], zr_sem.at[t, k - 1],
                {"col": lax.rem(z + k, cols)}))
    for cp in z_copies[0]:
        cp.start()
    for cp in z_copies[0]:
        cp.wait_recv()
    for cp in z_copies[1]:
        cp.start()
    out_copies = [pltpu.make_async_copy(x_all, x_out, xo_sem.at[0])]
    out_copies[0].start()

    sent = list(z_copies[0]) + list(z_copies[1])
    pair, chip_copies, gathers, forwards = {}, {}, {}, {}
    tile = cw // 3

    def stage_a(i):
        t, j = divmod(i, PARTS)
        loads[i].wait()
        if t == 0:
            @pl.loop(0, 3)
            def _(n):
                at = pl.ds(pl.multiple_of(n * tile, 128), tile)
                part[i, :, at] = times(x_all[...], wu[j, :, at]).astype(BF16)
        else:
            if j == 0:
                for cp in z_copies[1]:
                    cp.wait_recv()
                out_copies.append(
                    pltpu.make_async_copy(cot_all, cot_out, xo_sem.at[1]))
                out_copies[-1].start()

            @pl.loop(0, 3)
            def _(n):
                at = pl.ds(pl.multiple_of(n * tile, 128), tile)
                part[i, :, at] = times_transposed(
                    cot_all[...], wd[j, at, :]).astype(BF16)
        there = pl.ds(pl.multiple_of((1 - core) * half, 16), half)
        cp = send(part.at[i, there, :], pair_in.at[i], ps_sem.at[i], pr_sem.at[i],
                  partner)
        cp.start()
        pair[i] = cp
        sent.append(cp)

    def pair_total(i, where):
        low = pl.ds(pl.multiple_of(where * own, 16), own)
        return (part[i, block(core, where), :].astype(F32)
                + pair_in[i, low, :].astype(F32))

    def stage_b(i):
        pair[i].wait_recv()
        chip_copies[i] = []
        for k in range(1, chips):
            pair_sum[i, k - 1, :, :] = pair_total(i, peer_chip(k)).astype(BF16)
            cp = send(pair_sum.at[i, k - 1], chip_in.at[i, k - 1],
                      cs_sem.at[i, k - 1], cr_sem.at[i, k - 1], peer(k))
            cp.start()
            chip_copies[i].append(cp)
            sent.append(cp)

    def stage_c(i):
        t, j = divmod(i, PARTS)
        total = pair_total(i, chip)
        for k in range(1, chips):
            chip_copies[i][k - 1].wait_recv()
            total = total + chip_in[i, k - 1, :, :].astype(F32)
        here = block(core, chip)
        if t == 0:
            preact[j, :, :] = total
            gathered[i, here, :] = gelu_value(total).astype(BF16)
        else:
            gathered[i, here, :] = (total * gelu_slope(preact[j, :, :])).astype(BF16)
        gathers[i], forwards[i] = [], []
        mine_ref = gathered.at[i, here, :]
        for k in range(1, chips):
            cp = send(mine_ref, mine_ref, gs_sem.at[i, k - 1], gr_sem.at[i, k - 1],
                      peer(k))
            cp.start()
            gathers[i].append(cp)
            sent.append(cp)
        cp = send(mine_ref, mine_ref, fs_sem.at[i, 0], fr_sem.at[i, 0], partner)
        cp.start()
        forwards[i].append(cp)
        sent.append(cp)

    def stage_d(i):
        for k in range(1, chips):
            gathers[i][k - 1].wait_recv()
            ref = gathered.at[i, block(core, source_chip(k)), :]
            cp = send(ref, ref, fs_sem.at[i, k], fr_sem.at[i, k], partner)
            cp.start()
            forwards[i].append(cp)
            sent.append(cp)

    wtile = width // 3

    def stage_e(i):
        t, j = divmod(i, PARTS)
        for cp in forwards[i]:
            cp.wait_recv()
        target = act_out if t == 0 else pg_out
        cp = pltpu.make_async_copy(
            gathered.at[i], target.at[:, pl.ds(j * cw, cw)], o_sem.at[i])
        cp.start()
        out_copies.append(cp)

        @pl.loop(0, 3)
        def _(n):
            at = pl.ds(pl.multiple_of(n * wtile, 128), wtile)
            if t == 0:
                term = times(gathered[i], wd[j, :, at])
            else:
                term = times_transposed(gathered[i], wu[j, at, :])
            if j > 0:
                term = term + z_sum[t, :, at]
            if j < PARTS - 1:
                z_sum[t, :, at] = term
            else:
                z_low[t, :, at] = term.astype(BF16)

        if j == PARTS - 1:
            cp = pltpu.make_async_copy(z_low.at[t], z_out.at[t], xo_sem.at[2 + t])
            cp.start()
            out_copies.append(cp)

    stages = (stage_a, stage_b, stage_c, stage_d, stage_e)
    for step in range(items + len(stages) - 1):
        for lag, stage in enumerate(stages):
            if 0 <= step - lag < items:
                stage(step - lag)

    for cp in sent:
        cp.wait_send()
    for cp in out_copies:
        cp.wait()


def per_device(rows, cols, inputs, up_weight, down_weight, cotangent):
    share, width = inputs.shape
    hidden = up_weight.shape[1]
    tokens = share * cols
    chips = rows // 2
    items = 2 * PARTS
    cw = hidden // PARTS
    own = tokens // rows
    dma = pltpu.SemaphoreType.DMA
    anywhere = pl.BlockSpec(memory_space=pl.ANY)
    in_vmem = pl.BlockSpec(memory_space=pltpu.VMEM)

    activ, pregrad, all_inputs, all_cotangent, partial = pl.pallas_call(
        functools.partial(layer_kernel, rows, cols),
        out_shape=(
            jax.ShapeDtypeStruct((tokens, hidden), BF16),
            jax.ShapeDtypeStruct((tokens, hidden), BF16),
            jax.ShapeDtypeStruct((tokens, width), BF16),
            jax.ShapeDtypeStruct((tokens, width), BF16),
            jax.ShapeDtypeStruct((2, tokens, width), BF16),
        ),
        in_specs=[in_vmem, anywhere, anywhere, in_vmem],
        out_specs=(anywhere,) * 5,
        scratch_shapes=[
            pltpu.VMEM((tokens, width), BF16),
            pltpu.VMEM((tokens, width), BF16),
            pltpu.VMEM((PARTS, width, cw), BF16),
            pltpu.VMEM((PARTS, cw, width), BF16),
            pltpu.VMEM((items, tokens, cw), BF16),
            pltpu.VMEM((items, tokens // 2, cw), BF16),
            pltpu.VMEM((items, chips - 1, own, cw), BF16),
            pltpu.VMEM((items, chips - 1, own, cw), BF16),
            pltpu.VMEM((PARTS, own, cw), F32),
            pltpu.VMEM((items, tokens, cw), BF16),
            pltpu.VMEM((2, tokens, width), F32),
            pltpu.VMEM((2, tokens, width), BF16),
            dma((2, PARTS)),
            dma((2, cols - 1)),
            dma((2, cols - 1)),
            dma((items,)),
            dma((items,)),
            dma((items, chips - 1)),
            dma((items, chips - 1)),
            dma((items, chips - 1)),
            dma((items, chips - 1)),
            dma((items, chips)),
            dma((items, chips)),
            dma((items,)),
            dma((4,)),
        ],
        compiler_params=pltpu.CompilerParams(
            collective_id=0, has_side_effects=True, vmem_limit_bytes=58 * 2**20),
        cost_estimate=pl.CostEstimate(
            flops=8 * tokens * width * hidden,
            bytes_accessed=4 * width * hidden,
            transcendentals=2 * own * hidden),
    )(inputs, up_weight, down_weight, cotangent)

    me = lax.axis_index("col")

    def piece(k):
        start = lax.rem(me + k, cols) * share
        return lax.dynamic_slice_in_dim(partial, start, share, axis=1)

    arrived = [
        lax.ppermute(piece(k), "col", [(s, (s + k) % cols) for s in range(cols)])
        for k in range(1, cols)
    ]
    down_grad = over_tokens(activ, all_cotangent).astype(BF16)
    up_grad = over_tokens(all_inputs, pregrad).astype(BF16)
    total = piece(0).astype(F32)
    for other in arrived:
        total = total + other.astype(F32)
    total = total.astype(BF16)
    return (total[0], total[1], up_grad, down_grad)


def solution(mesh):
    placed = (P("col", "row"), P("row", "col"), P("col", "row"), P("col", "row"))
    return jax.shard_map(
        functools.partial(per_device, mesh.shape["row"], mesh.shape["col"]),
        mesh=mesh,
        in_specs=placed,
        out_specs=(P("col", "row"), P("col", "row"), P("row", "col"), P("col", "row")),
        check_vma=False,
    )
```

time: 262 us -> 92.5 us (0.35)
  waiting for transfers between devices: 116 us -> 0.01 us
  Pallas kernels: 0 us -> 62.5 us
  matrix products: 68.3 us -> 20.2 us
  blocking collectives: 31.9 us -> 0 us
  local copies, waits for them, and re-layouts: 24.8 us -> 2 us
  between operations: 14.1 us -> 0.69 us
  starting transfers between devices: 0.42 us -> 5.86 us
  other arithmetic: 5.28 us -> 1.04 us
    reduce_scatter x4 -> x0, waiting for transfers between devices: 72.6 us -> none  [the longest x1 50.6 us: per_device(): lax.psum_scatter(jnp.dot(all_inputs, up_weight, preferred_element_type=jn...]
    pallas_call x0 -> x1, Pallas kernels: none -> 62.5 us  [per_device(): pl.pallas_call(functools.partial(layer_kernel, rows, cols), out_shape=(ja...]
    dot_general x4 -> x0, matrix products: 49.3 us -> none  [the longest x2 28.3 us: times_transposed(): lax.dot_general(left, right, (((1,), (1,)), ((), ())), preferred_element_...]
    all_gather x2 -> x0, waiting for transfers between devices: 42.8 us -> none  [the longest x1 25.4 us: per_device(): all_activ = lax.all_gather(activ, 'row', axis=0, tiled=True)]
    all_gather x2 -> x0, blocking collectives: 31.9 us -> none  [the longest x1 16.4 us: per_device(): all_cotangent = lax.all_gather(cotangent, 'col', axis=0, tiled=True)]
    unnamed x7 -> x4, local copies, waits for them, and re-layouts: 24.8 us -> 0.01 us
    ppermute x0 -> x3, starting transfers between devices: none -> 5.86 us  [per_device(): lax.ppermute(piece(k), 'col', [(s, (s + k) % cols) for s in range(cols)])]
    convert_element_type x3 -> x1, other arithmetic: 5.28 us -> 1.04 us  [per_device(): total = total.astype(BF16)]
  transfers between devices with their start and end apart: 6 -> 3, of which waited for: 4 -> 0; matrix products, arithmetic and copies ran while one was open for 31% -> 22% of each run, Pallas kernels for 0% -> 0%
where the time goes in v1:
time: 92.5 us; the launch traced here: 92.3 us
  Pallas kernels  62.5 us (68%)
  matrix products  20.2 us (22%)
  starting transfers between devices  5.86 us (6%)
  local copies, waits for them, and re-layouts  2 us (2%)
  other arithmetic  1.04 us (1%)
    pallas_call x1, Pallas kernels, per_device(): pl.pallas_call(functools.partial(layer_kernel, rows, cols), out_shape=(ja...  62.5 us
    dot_general x2, matrix products, over_tokens(): lax.dot_general(left, right, (((0,), (0,)), ((), ())), preferred_element_...  20.2 us
    ppermute x3, starting transfers between devices, per_device(): lax.ppermute(piece(k), 'col', [(s, (s + k) % cols) for s in range(cols)])  5.86 us
  transfers between devices with their start and end apart: 3, of which 0 were waited for; matrix products, arithmetic and copies ran while one was open for 22% of the time, Pallas kernels for 0%

profile of v1, /device:TPU:0, one launch (start us, length us, event | category | flops | bytes accessed | tf_op | source)
XLA Modules:
  0.0 92.3 jit_solution(16956798489410144410)
XLA Ops:
  0.7 62.5 %shard_map.75 = (bf16[128,6144]{1,0:T(8,128)(2,1)}, bf16[128,6144]{1,0:T(8,128)(2,1)}, bf16[128,1536]{1,0:T(8,128)(2,1)}, bf16[128,1536]{1,0:T(8,128)(2,1)}, bf16[2,128,1536]{2,1,0:T(8,128)(2,1)}) custom-call(bf16[32,1536]{1,0:T(8,128)(2,1)} %x_ref.1, bf16[1536,6144]{1,0:T(8,128)(2,1)} %up_ref.1, bf16[6144,1536]{1,0:T(8,128)(2,1)} %down_ref.1, ...), custom_call_target="tpu_custom_call" | custom-call | flops 9663676416 | bytes 37748736 | tf_op jit(solution)/shard_map/pallas_call | solution.py:261
  63.1 0.0 copy-start
  63.1 0.0 copy-start.1
  63.2 1.3 %constant_dynamic-slice_fusion.2 = (bf16[2,32,1536]{2,1,0:T(8,128)(2,1)S(1)}, bf16[2,32,1536]{2,1,0:T(8,128)(2,1)S(1)}, bf16[2,32,1536]{2,1,0:T(8,128)(2,1)S(1)}) fusion(bf16[2,128,1536]{2,1,0:T(8,128)(2,1)} %get-tuple-element.9, s32[]{:T(128)S(6)} %select_n.13, s32[]{:T(128)S(6)} %select_n.15, s32[]{:T(128)S(6)} %select_n.14), kind=kLoop, calls=%fused_computation.7 | loop fusion | bytes 1179660 | tf_op jit(solution)/shard_map/dynamic_slice | solution.py:311
  64.5 4.3 %collective-permute-start = (bf16[2,32,1536]{2,1,0:T(8,128)(2,1)S(1)}, bf16[2,32,1536]{2,1,0:T(8,128)(2,1)S(1)}, u32[]{:S(2)}, u32[]{:S(2)}) collective-permute-start(bf16[2,32,1536]{2,1,0:T(8,128)(2,1)S(1)} %get-tuple-element.14), channel_id=1, source_target_pairs={{0,1},{1,2},{2,3},{3,0},{4,5},{5,6},{6,7},{7,4},{8,9},{9,10},{10,1... | collective-permute-start | bytes 589832 | tf_op jit(solution)/shard_map/ppermute | solution.py:314
  68.8 0.4 collective-permute-start.2
  69.2 1.1 %collective-permute-start.1 = (bf16[2,32,1536]{2,1,0:T(8,128)(2,1)S(1)}, bf16[2,32,1536]{2,1,0:T(8,128)(2,1)S(1)}, u32[]{:S(2)}, u32[]{:S(2)}) collective-permute-start(bf16[2,32,1536]{2,1,0:T(8,128)(2,1)S(1)} %get-tuple-element.16), channel_id=1, source_target_pairs={{0,2},{1,3},{2,0},{3,1},{4,6},{5,7},{6,4},{7,5},{8,10},{9,11},{10,... | collective-permute-start | bytes 589832 | tf_op jit(solution)/shard_map/ppermute | solution.py:314
  70.3 10.7 %convolution_convert_fusion = bf16[6144,1536]{1,0:T(8,128)(2,1)} fusion(bf16[128,6144]{1,0:T(8,128)(2,1)} %get-tuple-element.12, bf16[128,1536]{1,0:T(8,128)(2,1)} %get-tuple-element.13), kind=kOutput, calls=%fused_computation | convolution fusion | flops 2425356288 | bytes 20840448 | tf_op jit(solution)/shard_map/dot_general | solution.py:40
  81.0 0.0 copy-done
  81.0 0.0 copy-done.1
  81.0 9.5 %convolution_convert_fusion.1 = bf16[1536,6144]{1,0:T(8,128)(2,1)} fusion(bf16[128,1536]{1,0:T(8,128)(2,1)S(1)} %copy-done.1, bf16[128,6144]{1,0:T(8,128)(2,1)S(1)} %copy-done), kind=kOutput, calls=%fused_computation.1 | convolution fusion | flops 2425356288 | bytes 20840448 | tf_op jit(solution)/shard_map/dot_general | solution.py:40
  90.5 0.0 collective-permute-done
  90.6 0.0 collective-permute-done.2
  90.6 0.0 collective-permute-done.1
  90.6 1.0 %add_convert_fusion = bf16[2,32,1536]{2,1,0:T(8,128)(2,1)S(1)} fusion(bf16[2,32,1536]{2,1,0:T(8,128)(2,1)S(1)} %collective-permute-done.2, bf16[2,32,1536]{2,1,0:T(8,128)(2,1)S(1)} %collective-permute-done.1, bf16[2,32,1536]{2,1,0:T(8,128)(2,1)S(1)} %collective-permute-done, bf16[2,128,1536]{2,1,0:T(8,128)(2,1)} %get-tuple-element.9, s32[]{:T(128)S(6)} %select_n.12), kind=kLoop, calls=%fused_computation.2 | loop fusion | flops 786432 | bytes 983044 | tf_op jit(solution)/shard_map/convert_element_type | solution.py:322
  91.6 0.7 slice_bitcast_fusion
Async XLA Ops:
  63.1 17.9 %copy-start = (bf16[128,6144]{1,0:T(8,128)(2,1)S(1)}, bf16[128,6144]{1,0:T(8,128)(2,1)}, u32[]{:S(2)}) copy-start(bf16[128,6144]{1,0:T(8,128)(2,1)} %get-tuple-element.11) | copy-start | bytes 4718596
  63.1 17.9 %copy-start.1 = (bf16[128,1536]{1,0:T(8,128)(2,1)S(1)}, bf16[128,1536]{1,0:T(8,128)(2,1)}, u32[]{:S(2)}) copy-start(bf16[128,1536]{1,0:T(8,128)(2,1)} %get-tuple-element.10) | copy-start | bytes 1179652
  64.5 26.1 %collective-permute-start = (bf16[2,32,1536]{2,1,0:T(8,128)(2,1)S(1)}, bf16[2,32,1536]{2,1,0:T(8,128)(2,1)S(1)}, u32[]{:S(2)}, u32[]{:S(2)}) collective-permute-start(bf16[2,32,1536]{2,1,0:T(8,128)(2,1)S(1)} %get-tuple-element.14), channel_id=1, source_target_pairs={{0,1},{1,2},{2,3},{3,0},{4,5},{5,6},{6,7},{7,4},{8,9},{9,10},{10,1... | collective-permute-start | bytes 589832 | tf_op jit(solution)/shard_map/ppermute | solution.py:314
  68.8 21.8 %collective-permute-start.2 = (bf16[2,32,1536]{2,1,0:T(8,128)(2,1)S(1)}, bf16[2,32,1536]{2,1,0:T(8,128)(2,1)S(1)}, u32[]{:S(2)}, u32[]{:S(2)}) collective-permute-start(bf16[2,32,1536]{2,1,0:T(8,128)(2,1)S(1)} %get-tuple-element.15), channel_id=1, source_target_pairs={{0,3},{1,0},{2,1},{3,2},{4,7},{5,4},{6,5},{7,6},{8,11},{9,8},{10,9... | collective-permute-start | bytes 589832 | tf_op jit(solution)/shard_map/ppermute | solution.py:314
  69.2 21.3 %collective-permute-start.1 = (bf16[2,32,1536]{2,1,0:T(8,128)(2,1)S(1)}, bf16[2,32,1536]{2,1,0:T(8,128)(2,1)S(1)}, u32[]{:S(2)}, u32[]{:S(2)}) collective-permute-start(bf16[2,32,1536]{2,1,0:T(8,128)(2,1)S(1)} %get-tuple-element.16), channel_id=1, source_target_pairs={{0,2},{1,3},{2,0},{3,1},{4,6},{5,7},{6,4},{7,5},{8,10},{9,11},{10,... | collective-permute-start | bytes 589832 | tf_op jit(solution)/shard_map/ppermute | solution.py:314

commit v2 on v1

--- a/solution.py
+++ b/solution.py
@@ -45,12 +45,13 @@
 def layer_kernel(
     rows, cols,
     x_ref, up_ref, down_ref, cot_ref,
-    act_out, pg_out, x_out, cot_out, z_out,
-    x_all, cot_all, wu, wd, part, pair_in, pair_sum, chip_in, preact, gathered,
+    act_out, pg_out, x_out, cot_out, *rest,
+):
+    z_outs = rest[:cols]
+    (x_all, cot_all, wu, wd, part, pair_in, pair_sum, chip_in, preact, gathered,
     z_sum, z_low,
     w_sem, zs_sem, zr_sem, ps_sem, pr_sem, cs_sem, cr_sem, gs_sem, gr_sem,
-    fs_sem, fr_sem, o_sem, xo_sem,
-):
+    fs_sem, fr_sem, o_sem, xo_sem, zo_sem) = rest[cols:]
     chips = rows // 2
     tokens, width = x_all.shape
     share = x_ref.shape[0]
@@ -132,7 +133,7 @@
             @pl.loop(0, 3)
             def _(n):
                 at = pl.ds(pl.multiple_of(n * tile, 128), tile)
-                part[i, :, at] = times(x_all[...], wu[j, :, at]).astype(BF16)
+                part[i, :, at] = times(x_all[...], wu[j, :, at])
         else:
             if j == 0:
                 for cp in z_copies[1]:
@@ -144,8 +145,7 @@
             @pl.loop(0, 3)
             def _(n):
                 at = pl.ds(pl.multiple_of(n * tile, 128), tile)
-                part[i, :, at] = times_transposed(
-                    cot_all[...], wd[j, at, :]).astype(BF16)
+                part[i, :, at] = times_transposed(cot_all[...], wd[j, at, :])
         there = pl.ds(pl.multiple_of((1 - core) * half, 16), half)
         cp = send(part.at[i, there, :], pair_in.at[i], ps_sem.at[i], pr_sem.at[i],
                   partner)
@@ -155,8 +155,7 @@
 
     def pair_total(i, where):
         low = pl.ds(pl.multiple_of(where * own, 16), own)
-        return (part[i, block(core, where), :].astype(F32)
-                + pair_in[i, low, :].astype(F32))
+        return part[i, block(core, where), :] + pair_in[i, low, :]
 
     def stage_b(i):
         pair[i].wait_recv()
@@ -230,9 +229,13 @@
                 z_low[t, :, at] = term.astype(BF16)
 
         if j == PARTS - 1:
-            cp = pltpu.make_async_copy(z_low.at[t], z_out.at[t], xo_sem.at[2 + t])
-            cp.start()
-            out_copies.append(cp)
+            for k in range(cols):
+                rows_k = pl.ds(
+                    pl.multiple_of(lax.rem(z + k, cols) * share, 16), share)
+                cp = pltpu.make_async_copy(
+                    z_low.at[t, rows_k, :], z_outs[k].at[t], zo_sem.at[t, k])
+                cp.start()
+                out_copies.append(cp)
 
     stages = (stage_a, stage_b, stage_c, stage_d, stage_e)
     for step in range(items + len(stages) - 1):
@@ -244,6 +247,51 @@
         cp.wait_send()
     for cp in out_copies:
         cp.wait()
+
+
+def grads_kernel(x_ref, cot_ref, act_ref, pg_ref, up_out, down_out, x_turned):
+    @pl.when(pl.program_id(0) == 0)
+    def _():
+        x_turned[...] = x_ref[...].T
+
+    width = x_ref.shape[1]
+    rows_at_once = width // 6
+    for n in range(6):
+        at = pl.ds(n * rows_at_once, rows_at_once)
+        up_out[at, :] = times(x_turned[at, :], pg_ref[...]).astype(BF16)
+    acts = act_ref[...].T
+    down_cols = width // 3
+    for n in range(3):
+        at = pl.ds(n * down_cols, down_cols)
+        down_out[:, at] = times(acts, cot_ref[:, at]).astype(BF16)
+
+
+def weight_grads(inputs, cotangent, activ, pregrad):
+    tokens, width = inputs.shape
+    hidden = activ.shape[1]
+    steps = width // 128
+    span = hidden // steps
+    fixed = pl.BlockSpec((tokens, width), lambda i: (0, 0))
+    moving = pl.BlockSpec((tokens, span), lambda i: (0, i))
+    return pl.pallas_call(
+        grads_kernel,
+        grid=(steps,),
+        out_shape=(
+            jax.ShapeDtypeStruct((width, hidden), BF16),
+            jax.ShapeDtypeStruct((hidden, width), BF16),
+        ),
+        in_specs=[fixed, fixed, moving, moving],
+        out_specs=(
+            pl.BlockSpec((width, span), lambda i: (0, i)),
+            pl.BlockSpec((span, width), lambda i: (i, 0)),
+        ),
+        scratch_shapes=[pltpu.VMEM((width, tokens), BF16)],
+        compiler_params=pltpu.CompilerParams(vmem_limit_bytes=32 * 2**20),
+        cost_estimate=pl.CostEstimate(
+            flops=4 * tokens * width * hidden,
+            bytes_accessed=4 * width * hidden,
+            transcendentals=0),
+    )(inputs, cotangent, activ, pregrad)
 
 
 def per_device(rows, cols, inputs, up_weight, down_weight, cotangent):
@@ -258,24 +306,23 @@
     anywhere = pl.BlockSpec(memory_space=pl.ANY)
     in_vmem = pl.BlockSpec(memory_space=pltpu.VMEM)
 
-    activ, pregrad, all_inputs, all_cotangent, partial = pl.pallas_call(
+    activ, pregrad, all_inputs, all_cotangent, *pieces = pl.pallas_call(
         functools.partial(layer_kernel, rows, cols),
         out_shape=(
             jax.ShapeDtypeStruct((tokens, hidden), BF16),
             jax.ShapeDtypeStruct((tokens, hidden), BF16),
             jax.ShapeDtypeStruct((tokens, width), BF16),
             jax.ShapeDtypeStruct((tokens, width), BF16),
-            jax.ShapeDtypeStruct((2, tokens, width), BF16),
-        ),
+        ) + (jax.ShapeDtypeStruct((2, share, width), BF16),) * cols,
         in_specs=[in_vmem, anywhere, anywhere, in_vmem],
-        out_specs=(anywhere,) * 5,
+        out_specs=(anywhere,) * (4 + cols),
         scratch_shapes=[
             pltpu.VMEM((tokens, width), BF16),
             pltpu.VMEM((tokens, width), BF16),
             pltpu.VMEM((PARTS, width, cw), BF16),
             pltpu.VMEM((PARTS, cw, width), BF16),
-            pltpu.VMEM((items, tokens, cw), BF16),
-            pltpu.VMEM((items, tokens // 2, cw), BF16),
+            pltpu.VMEM((items, tokens, cw), F32),
+            pltpu.VMEM((items, tokens // 2, cw), F32),
             pltpu.VMEM((items, chips - 1, own, cw), BF16),
             pltpu.VMEM((items, chips - 1, own, cw), BF16),
             pltpu.VMEM((PARTS, own, cw), F32),
@@ -294,7 +341,8 @@
             dma((items, chips)),
             dma((items, chips)),
             dma((items,)),
-            dma((4,)),
+            dma((2,)),
+            dma((2, cols)),
         ],
         compiler_params=pltpu.CompilerParams(
             collective_id=0, has_side_effects=True, vmem_limit_bytes=58 * 2**20),
@@ -304,23 +352,19 @@
             transcendentals=2 * own * hidden),
     )(inputs, up_weight, down_weight, cotangent)
 
-    me = lax.axis_index("col")
-
-    def piece(k):
-        start = lax.rem(me + k, cols) * share
-        return lax.dynamic_slice_in_dim(partial, start, share, axis=1)
-
     arrived = [
-        lax.ppermute(piece(k), "col", [(s, (s + k) % cols) for s in range(cols)])
+        lax.ppermute(pieces[k], "col", [(s, (s + k) % cols) for s in range(cols)])
         for k in range(1, cols)
     ]
-    down_grad = over_tokens(activ, all_cotangent).astype(BF16)
-    up_grad = over_tokens(all_inputs, pregrad).astype(BF16)
-    total = piece(0).astype(F32)
-    for other in arrived:
-        total = total + other.astype(F32)
-    total = total.astype(BF16)
-    return (total[0], total[1], up_grad, down_grad)
+    up_grad, down_grad = weight_grads(all_inputs, all_cotangent, activ, pregrad)
+
+    def total(t):
+        terms = pieces[0][t].astype(F32)
+        for other in arrived:
+            terms = terms + other[t].astype(F32)
+        return terms.astype(BF16)
+
+    return (total(0), total(1), up_grad, down_grad)
 
 
 def solution(mesh):

time: 92.5 us -> 91.3 us (0.987)
  matrix products: 20.2 us -> 0 us
  Pallas kernels: 62.5 us -> 76.9 us
  local copies, waits for them, and re-layouts: 2 us -> 4.81 us
  starting transfers between devices: 5.86 us -> 6.84 us
    dot_general x2 -> x0, matrix products: 20.2 us -> none  [over_tokens(): lax.dot_general(left, right, (((0,), (0,)), ((), ())), preferred_element_...]
    pallas_call x0 -> x1, Pallas kernels: none -> 14.4 us  [weight_grads(): pl.pallas_call(grads_kernel, grid=(steps,), out_shape=(jax.ShapeDtypeStru...]
    unnamed x4 -> x8, local copies, waits for them, and re-layouts: 0.01 us -> 4.81 us
    add x0 -> x1, other arithmetic: none -> 1.71 us  [total(): terms = terms + other[t].astype(F32)]
    dynamic_slice x1 -> x0, local copies, waits for them, and re-layouts: 1.31 us -> none  [piece(): return lax.dynamic_slice_in_dim(partial, start, share, axis=1)]
    convert_element_type x1 -> x0, other arithmetic: 1.04 us -> none  [per_device(): total = total.astype(BF16)]
    ppermute x3, starting transfers between devices: 5.86 us -> 6.84 us  [per_device(): lax.ppermute(pieces[k], 'col', [(s, (s + k) % cols) for s in range(cols)])]
  transfers between devices with their start and end apart: 3 -> 3, of which waited for: 0 -> 0; matrix products, arithmetic and copies ran while one was open for 22% -> 0% of each run, Pallas kernels for 0% -> 16%
where the time goes in v2:
time: 91.3 us; the launch traced here: 90.9 us
  Pallas kernels  76.9 us (84%)
  starting transfers between devices  6.84 us (7%)
  local copies, waits for them, and re-layouts  4.81 us (5%)
  other arithmetic  1.71 us (2%)
    pallas_call x1, Pallas kernels, per_device(): pl.pallas_call(functools.partial(layer_kernel, rows, cols), out_shape=(ja...  62.5 us
    pallas_call x1, Pallas kernels, weight_grads(): pl.pallas_call(grads_kernel, grid=(steps,), out_shape=(jax.ShapeDtypeStru...  14.4 us
    ppermute x3, starting transfers between devices, per_device(): lax.ppermute(pieces[k], 'col', [(s, (s + k) % cols) for s in range(cols)])  6.84 us
    unnamed x8, local copies, waits for them, and re-layouts  4.81 us
  transfers between devices with their start and end apart: 3, of which 0 were waited for; matrix products, arithmetic and copies ran while one was open for 0% of the time, Pallas kernels for 16%

profile of v2, /device:TPU:0, one launch (start us, length us, event | category | flops | bytes accessed | tf_op | source)
XLA Modules:
  0.0 90.9 jit_solution(18131649980025556397)
XLA Ops:
  0.6 62.5 %shard_map.75 = (bf16[128,6144]{1,0:T(8,128)(2,1)}, bf16[128,6144]{1,0:T(8,128)(2,1)}, bf16[128,1536]{1,0:T(8,128)(2,1)}, bf16[128,1536]{1,0:T(8,128)(2,1)}, bf1...) custom-call(bf16[32,1536]{1,0:T(8,128)(2,1)} %x_ref.1, ...), custom_call_target="tpu_custom_call" | custom-call | flops 9663676416 | bytes 37748736 | tf_op jit(solution)/shard_map/pallas_call | solution.py:309
  63.2 4.4 %collective-permute-start = (bf16[2,32,1536]{2,1,0:T(8,128)(2,1)}, bf16[2,32,1536]{2,1,0:T(8,128)(2,1)S(1)}, u32[]{:S(2)}, u32[]{:S(2)}) collective-permute-start(bf16[2,32,1536]{2,1,0:T(8,128)(2,1)} %get-tuple-element.15), channel_id=1, source_target_pairs={{0,1},{1,2},{2,3},{3,0},{4,5},{5,6},{6,7},{7,4},{8,9},{9,10},{10,1... | collective-permute-start | bytes 589832 | tf_op jit(solution)/shard_map/ppermute | solution.py:356
  67.6 1.0 %collective-permute-start.1 = (bf16[2,32,1536]{2,1,0:T(8,128)(2,1)}, bf16[2,32,1536]{2,1,0:T(8,128)(2,1)S(1)}, u32[]{:S(2)}, u32[]{:S(2)}) collective-permute-start(bf16[2,32,1536]{2,1,0:T(8,128)(2,1)} %get-tuple-element.16), channel_id=1, source_target_pairs={{0,2},{1,3},{2,0},{3,1},{4,6},{5,7},{6,4},{7,5},{8,10},{9,11},{10,... | collective-permute-start | bytes 589832 | tf_op jit(solution)/shard_map/ppermute | solution.py:356
  68.5 1.5 %collective-permute-start.2 = (bf16[2,32,1536]{2,1,0:T(8,128)(2,1)}, bf16[2,32,1536]{2,1,0:T(8,128)(2,1)S(1)}, u32[]{:S(2)}, u32[]{:S(2)}) collective-permute-start(bf16[2,32,1536]{2,1,0:T(8,128)(2,1)} %get-tuple-element.17), channel_id=1, source_target_pairs={{0,3},{1,0},{2,1},{3,2},{4,7},{5,4},{6,5},{7,6},{8,11},{9,8},{10,9... | collective-permute-start | bytes 589832 | tf_op jit(solution)/shard_map/ppermute | solution.py:356
  70.0 0.0 copy-start
  70.0 1.4 %copy-done = bf16[128,6144]{1,0:T(8,128)(2,1)S(1)} copy-done((bf16[128,6144]{1,0:T(8,128)(2,1)S(1)}, bf16[128,6144]{1,0:T(8,128)(2,1)}, u32[]{:S(2)}) %copy-start) | copy-done | bytes 1572888
  71.4 0.0 copy-start.1
  71.4 1.4 %copy-done.1 = bf16[128,6144]{1,0:T(8,128)(2,1)S(1)} copy-done((bf16[128,6144]{1,0:T(8,128)(2,1)S(1)}, bf16[128,6144]{1,0:T(8,128)(2,1)}, u32[]{:S(2)}) %copy-start.1) | copy-done | bytes 1572888
  72.8 0.0 copy-start.2
  72.8 1.0 %copy-done.2 = bf16[128,1536]{1,0:T(8,128)(2,1)S(1)} copy-done((bf16[128,1536]{1,0:T(8,128)(2,1)S(1)}, bf16[128,1536]{1,0:T(8,128)(2,1)}, u32[]{:S(2)}) %copy-start.2) | copy-done | bytes 393240
  73.8 0.0 copy-start.3
  73.8 1.0 %copy-done.3 = bf16[128,1536]{1,0:T(8,128)(2,1)S(1)} copy-done((bf16[128,1536]{1,0:T(8,128)(2,1)S(1)}, bf16[128,1536]{1,0:T(8,128)(2,1)}, u32[]{:S(2)}) %copy-start.3) | copy-done | bytes 393240
  74.8 14.4 %shard_map.76 = (bf16[1536,6144]{1,0:T(8,128)(2,1)}, bf16[6144,1536]{1,0:T(8,128)(2,1)}) custom-call(bf16[128,1536]{1,0:T(8,128)(2,1)S(1)} %copy-done.2, bf16[128,1536]{1,0:T(8,128)(2,1)S(1)} %copy-done.3, bf16[128,6144]{1,0:T(8,128)(2,1)S(1)} %copy-done, bf16[128,6144]{1,0:T(8,128)(2,1)S(1)} %copy-done.1), custom_call_target="tpu_custom_call" | custom-call | flops 4831838208 | bytes 37748736 | tf_op jit(solution)/shard_map/pallas_call | solution.py:276
  89.2 0.0 collective-permute-done
  89.2 0.0 collective-permute-done.1
  89.2 0.0 collective-permute-done.2
  89.2 1.7 %fusion.1 = (bf16[32,1536]{1,0:T(8,128)(2,1)}, bf16[32,1536]{1,0:T(8,128)(2,1)}) fusion(bf16[2,32,1536]{2,1,0:T(8,128)(2,1)S(1)} %collective-permute-done.2, bf16[2,32,1536]{2,1,0:T(8,128)(2,1)S(1)} %collective-permute-done.1, bf16[2,32,1536]{2,1,0:T(8,128)(2,1)S(1)} %collective-permute-done, bf16[2,32,1536]{2,1,0:T(8,128)(2,1)} %get-tuple-element.14), kind=kLoop, calls=%fused_computation.3 | loop fusion | flops 786432 | bytes 983040 | tf_op jit(solution)/shard_map/add | solution.py:364
Async XLA Ops:
  63.2 26.0 %collective-permute-start = (bf16[2,32,1536]{2,1,0:T(8,128)(2,1)}, bf16[2,32,1536]{2,1,0:T(8,128)(2,1)S(1)}, u32[]{:S(2)}, u32[]{:S(2)}) collective-permute-start(bf16[2,32,1536]{2,1,0:T(8,128)(2,1)} %get-tuple-element.15), channel_id=1, source_target_pairs={{0,1},{1,2},{2,3},{3,0},{4,5},{5,6},{6,7},{7,4},{8,9},{9,10},{10,1... | collective-permute-start | bytes 589832 | tf_op jit(solution)/shard_map/ppermute | solution.py:356
  67.6 21.7 %collective-permute-start.1 = (bf16[2,32,1536]{2,1,0:T(8,128)(2,1)}, bf16[2,32,1536]{2,1,0:T(8,128)(2,1)S(1)}, u32[]{:S(2)}, u32[]{:S(2)}) collective-permute-start(bf16[2,32,1536]{2,1,0:T(8,128)(2,1)} %get-tuple-element.16), channel_id=1, source_target_pairs={{0,2},{1,3},{2,0},{3,1},{4,6},{5,7},{6,4},{7,5},{8,10},{9,11},{10,... | collective-permute-start | bytes 589832 | tf_op jit(solution)/shard_map/ppermute | solution.py:356
  68.5 20.7 %collective-permute-start.2 = (bf16[2,32,1536]{2,1,0:T(8,128)(2,1)}, bf16[2,32,1536]{2,1,0:T(8,128)(2,1)S(1)}, u32[]{:S(2)}, u32[]{:S(2)}) collective-permute-start(bf16[2,32,1536]{2,1,0:T(8,128)(2,1)} %get-tuple-element.17), channel_id=1, source_target_pairs={{0,3},{1,0},{2,1},{3,2},{4,7},{5,4},{6,5},{7,6},{8,11},{9,8},{10,9... | collective-permute-start | bytes 589832 | tf_op jit(solution)/shard_map/ppermute | solution.py:356
  70.0 1.4 %copy-start = (bf16[128,6144]{1,0:T(8,128)(2,1)S(1)}, bf16[128,6144]{1,0:T(8,128)(2,1)}, u32[]{:S(2)}) copy-start(bf16[128,6144]{1,0:T(8,128)(2,1)} %get-tuple-element.20.act_ref) | copy-start | bytes 4718596
  71.4 1.4 %copy-start.1 = (bf16[128,6144]{1,0:T(8,128)(2,1)S(1)}, bf16[128,6144]{1,0:T(8,128)(2,1)}, u32[]{:S(2)}) copy-start(bf16[128,6144]{1,0:T(8,128)(2,1)} %get-tuple-element.21.pg_ref) | copy-start | bytes 4718596
  72.8 1.0 %copy-start.2 = (bf16[128,1536]{1,0:T(8,128)(2,1)S(1)}, bf16[128,1536]{1,0:T(8,128)(2,1)}, u32[]{:S(2)}) copy-start(bf16[128,1536]{1,0:T(8,128)(2,1)} %get-tuple-element.18.x_ref) | copy-start | bytes 1179652
  73.8 1.0 %copy-start.3 = (bf16[128,1536]{1,0:T(8,128)(2,1)S(1)}, bf16[128,1536]{1,0:T(8,128)(2,1)}, u32[]{:S(2)}) copy-start(bf16[128,1536]{1,0:T(8,128)(2,1)} %get-tuple-element.19.cot_ref) | copy-start | bytes 1179652
